TPU v7x, 32 devices: a whole 2x2x4 slice. The times are simulated.
32 devices in a mesh: thinker: 4 (over z), seq: 8 (over y, x, core).
Axes of the slice: x: 2, y: 2, z: 4, core: 2. Of those that a mesh axis runs over, the one named last changes fastest.
Arguments:
- queries: bfloat16 [4, 1024, 2048], P('thinker', 'seq'), may hold values from -6 to 6
- keys: bfloat16 [4, 1024, 512], P('thinker', 'seq'), may hold values from -6 to 6
- values: bfloat16 [4, 1024, 512], P('thinker', 'seq'), may hold values from -6 to 6
- forward_out: bfloat16 [4, 1024, 2048], P('thinker', 'seq'), may hold values from -2 to 2
- logsumexp: float32 [4, 16, 1024], P('thinker', None, 'seq'), may hold values from -1 to 16, as said below
- upstream: bfloat16 [128, 32, 2048], P(None, ('thinker', 'seq')), may hold values from -6 to 6
- lengths: int32 [4], replicated, may hold values from 128 to 1024, as said below
- sibling_mask: int32 [4, 3, 8], P('thinker', None, 'seq'), may hold values from 0 to 1, as said below
Outputs:
- query_grad: bfloat16 [4, 1024, 2048], P('thinker', 'seq')
- key_grad: bfloat16 [4, 1024, 512], P('thinker', 'seq')
- value_grad: bfloat16 [4, 1024, 512], P('thinker', 'seq')
Inputs may be any that keep to these rules, and one draw needn't show every extreme that they name: lengths[t] valid positions stand at the start of thinker t's trace; two thinkers have exactly 1024, one exactly 128. sibling_mask[t, r, b] = 1 where query block b of thinker t reads the recent tokens of thinker (t + r + 1) % 4; the two thinkers of length 1024 read each other in the blocks of the last 128 positions. `logsumexp`: rows of positions past a trace's length carry arbitrary values.
All inputs are finite; a program needn't handle non-finite values.
Results may differ from a plain program's by a relative error of at most 0.014.
Values may be sent and summed in bfloat16 or wider, within the bound.
A program may use at most 128 MiB of HBM per device.

v0:
```python
import math

import jax
import jax.numpy as jnp
from jax import lax
from jax.sharding import PartitionSpec as P

BLOCK = 128


def from_behind(block, axis, distance):
    devices = range(lax.axis_size(axis))
    route = [(i - distance, i) for i in devices if i - distance in devices]
    return lax.ppermute(block, axis, route)


def pair_grads(
    query_heads, upstream_heads, lse_heads, delta_heads, key_rows, value_rows, allowed, factor
):
    count = key_rows.shape[0]
    kv_heads = query_heads.shape[1]
    head_dim = query_heads.shape[3]
    key_heads = key_rows.reshape(count, kv_heads, head_dim)
    value_heads = value_rows.reshape(count, kv_heads, head_dim)
    scores = (
        jnp.einsum("ikgd,jkd->kgij", query_heads, key_heads, preferred_element_type=jnp.float32)
        * factor
    )
    probs = jnp.where(allowed, jnp.exp(scores - lse_heads[..., None]), 0.0)
    dprobs = jnp.einsum(
        "ikgd,jkd->kgij", upstream_heads, value_heads, preferred_element_type=jnp.float32
    )
    dscores = probs * (dprobs - delta_heads[..., None])
    probs_low = probs.astype(jnp.bfloat16)
    dscores_low = dscores.astype(jnp.bfloat16)
    value_part = jnp.einsum(
        "kgij,ikgd->jkd", probs_low, upstream_heads, preferred_element_type=jnp.float32
    )
    key_part = (
        jnp.einsum("kgij,ikgd->jkd", dscores_low, query_heads, preferred_element_type=jnp.float32)
        * factor
    )
    query_part = (
        jnp.einsum("kgij,jkd->ikgd", dscores_low, key_heads, preferred_element_type=jnp.float32)
        * factor
    )
    rows = query_heads.shape[0]
    return (
        query_part.reshape(rows, -1),
        key_part.reshape(count, -1),
        value_part.reshape(count, -1),
    )


def shards(queries, keys, values, forward_out, logsumexp, upstream, lengths, sibling_mask):
    thinkers = lax.axis_size("thinker")
    seq_count = lax.axis_size("seq")
    devices = thinkers * seq_count
    rows = queries.shape[1]
    qwidth = queries.shape[2]
    kwidth = keys.shape[2]
    heads = logsumexp.shape[1]
    head_dim = qwidth // heads
    kv_heads = kwidth // head_dim
    group = heads // kv_heads
    factor = head_dim ** (-0.5)
    thinker = lax.axis_index("thinker")
    shard = lax.axis_index("seq")
    length = rows * seq_count
    per_peer = rows // devices
    arranged = upstream.reshape(devices, per_peer, 1, qwidth)
    arrived = lax.all_to_all(arranged, ("thinker", "seq"), split_axis=0, concat_axis=2, tiled=True)
    grad_out = arrived.reshape(rows, qwidth)
    query_heads = queries[0].reshape(rows, kv_heads, group, head_dim)
    upstream_heads = grad_out.reshape(rows, kv_heads, group, head_dim)
    output_heads = forward_out[0].reshape(rows, kv_heads, group, head_dim)
    delta = jnp.sum(upstream_heads.astype(jnp.float32) * output_heads.astype(jnp.float32), axis=-1)
    delta_heads = jnp.transpose(delta, (1, 2, 0))
    lse_heads = logsumexp[0].reshape(kv_heads, group, rows)
    my_length = lengths[thinker]
    first_query = shard * rows
    query_pos = first_query + jnp.arange(rows, dtype=jnp.int32)
    query_live = query_pos < my_length

    def own_block(key_rows, value_rows, key_start):
        count = key_rows.shape[0]
        key_pos = key_start + jnp.arange(count, dtype=jnp.int32)
        allowed = (
            (key_pos[None, :] <= query_pos[:, None])
            & query_live[:, None]
            & (key_pos[None, :] < my_length)
        )
        return pair_grads(
            query_heads,
            upstream_heads,
            lse_heads,
            delta_heads,
            key_rows,
            value_rows,
            allowed,
            factor,
        )

    whole_keys, whole_values = (
        lax.all_gather(keys, "seq", axis=1, tiled=True),
        lax.all_gather(values, "seq", axis=1, tiled=True),
    )
    whole_keys = whole_keys[0]
    whole_values = whole_values[0]
    width_block = math.gcd(length, 512)

    def add_query(position, total):
        start = position * width_block
        key_rows = lax.dynamic_slice_in_dim(whole_keys, start, width_block, 0)
        value_rows = lax.dynamic_slice_in_dim(whole_values, start, width_block, 0)
        return total + own_block(key_rows, value_rows, start)[0]

    query_total = lax.fori_loop(
        0, length // width_block, add_query, jnp.zeros((rows, qwidth), jnp.float32)
    )
    sub_rows = math.gcd(rows * lax.axis_size("seq"), 512)

    def one_block(position, buffer):
        key_start = position * sub_rows
        key_rows = lax.dynamic_slice_in_dim(whole_keys, key_start, sub_rows, 0)
        value_rows = lax.dynamic_slice_in_dim(whole_values, key_start, sub_rows, 0)
        parts = own_block(key_rows, value_rows, key_start)
        joined = jnp.concatenate([parts[1], parts[2]], axis=1)
        return lax.dynamic_update_slice_in_dim(buffer, joined, position * sub_rows, 0)

    own_grads = lax.psum_scatter(
        lax.fori_loop(
            0,
            rows * lax.axis_size("seq") // sub_rows,
            one_block,
            jnp.zeros((rows * lax.axis_size("seq"), 2 * kwidth), jnp.float32),
        ).astype(jnp.bfloat16),
        "seq",
        scatter_dimension=0,
        tiled=True,
    ).astype(jnp.float32)
    own_key = own_grads[:, :kwidth]
    own_value = own_grads[:, kwidth:]
    sibling_keys, sibling_values = (
        lax.all_gather(keys, "thinker", axis=0, tiled=True),
        lax.all_gather(values, "thinker", axis=0, tiled=True),
    )
    prior_keys, prior_values = from_behind((sibling_keys, sibling_values), "seq", 1)
    window_keys = jnp.roll(jnp.concatenate([prior_keys, sibling_keys], axis=1), -thinker, axis=0)
    window_values = jnp.roll(
        jnp.concatenate([prior_values, sibling_values], axis=1), -thinker, axis=0
    )
    key_pos = first_query - rows + jnp.arange(2 * rows, dtype=jnp.int32)
    near = (
        (key_pos[None, :] <= query_pos[:, None])
        & (key_pos[None, :] > query_pos[:, None] - rows)
        & (key_pos[None, :] >= 0)
        & query_live[:, None]
    )
    mask_rows = sibling_mask[0]
    key_terms_list = [jnp.zeros((2 * rows, kwidth), jnp.float32)]
    value_terms_list = [jnp.zeros((2 * rows, kwidth), jnp.float32)]
    for offset in range(1, thinkers):
        sibling = (thinker + offset) % thinkers
        visible = jnp.repeat(mask_rows[offset - 1], BLOCK) == 1
        allowed = near & visible[:, None] & (key_pos[None, :] < lengths[sibling])
        extra_query, extra_key, extra_value = pair_grads(
            query_heads,
            upstream_heads,
            lse_heads,
            delta_heads,
            window_keys[offset],
            window_values[offset],
            allowed,
            factor,
        )
        query_total = query_total + extra_query
        key_terms_list.append(extra_key)
        value_terms_list.append(extra_value)
    key_stack = jnp.roll(jnp.stack(key_terms_list), thinker, axis=0)
    value_stack = jnp.roll(jnp.stack(value_terms_list), thinker, axis=0)
    sibling_key, sibling_value = (
        lax.psum_scatter(
            key_stack.astype(jnp.bfloat16), "thinker", scatter_dimension=0, tiled=True
        ).astype(jnp.float32),
        lax.psum_scatter(
            value_stack.astype(jnp.bfloat16), "thinker", scatter_dimension=0, tiled=True
        ).astype(jnp.float32),
    )
    earlier_key, earlier_value = (
        from_behind(sibling_key[0, :rows].astype(jnp.bfloat16), "seq", -1).astype(jnp.float32),
        from_behind(sibling_value[0, :rows].astype(jnp.bfloat16), "seq", -1).astype(jnp.float32),
    )
    key_grad = (own_key + sibling_key[0, rows:] + earlier_key).astype(jnp.bfloat16)[None]
    value_grad = (own_value + sibling_value[0, rows:] + earlier_value).astype(jnp.bfloat16)[None]
    return (query_total.astype(jnp.bfloat16)[None], key_grad, value_grad)


def solution(mesh):
    placed = (
        P("thinker", "seq", None),
        P("thinker", "seq", None),
        P("thinker", "seq", None),
        P("thinker", "seq", None),
        P("thinker", None, "seq"),
        P(None, ("thinker", "seq"), None),
        P(),
        P("thinker", None, "seq"),
    )
    return jax.shard_map(
        shards,
        mesh=mesh,
        in_specs=placed,
        out_specs=(P("thinker", "seq", None), P("thinker", "seq", None), P("thinker", "seq", None)),
        check_vma=False,
    )
```

profile of v0, /device:TPU:11, one launch (start us, length us, event | category | flops | bytes accessed | tf_op | source)
XLA Modules:
  0.0 221.2 jit_solution(3947208645673061200)
XLA Ops:
  8.1 1.7 copy.166
  9.8 2.0 reshape.154
  11.8 6.4 %all-to-all-start = ((bf16[32,4,1,2048]{3,1,2,0:T(4,128)(2,1)}), bf16[32,4,1,2048]{3,1,2,0:T(4,128)(2,1)}, u32[]{:S(2)}, u32[]{:S(2)}) async-start(bf16[32,4,1,2048]{3,1,2,0:T(4,128)(2,1)} %reshape.154), calls=%async_computation | async-start | bytes 1048576 | tf_op jit(solution)/shard_map/all_to_all | solution.py:72
  18.3 21.5 %all_gather.15 = bf16[4,128,512]{2,1,0:T(8,128)(2,1)S(1)} all-gather(bf16[1,128,512]{2,1,0:T(8,128)(2,1)S(1)} %copy-done.19), channel_id=1, replica_groups=mesh['thinker'=4,'seq'=8] {'thinker'}, dimensions={0}, use_global_device_ids=true | all-gather | bytes 655360 | tf_op jit(solution)/shard_map/all_gather | solution.py:146
  40.1 6.3 %collective-permute-start.1 = (bf16[4,128,512]{1,2,0:T(8,128)(2,1)S(1)}, bf16[4,128,512]{1,2,0:T(8,128)(2,1)}, u32[]{:S(2)}, u32[]{:S(2)}) collective-permute-start(bf16[4,128,512]{1,2,0:T(8,128)(2,1)S(1)} %copy.179), channel_id=1, source_target_pairs={{0,1},{1,2},{2,3},{3,4},{4,5},{5,6},{6,7},{8,9},{9,10},{10,11},{11... | collective-permute-start | bytes 1572872 | tf_op jit(solution)/shard_map/ppermute | solution.py:14
  46.4 14.3 %all_gather.14 = bf16[4,128,512]{2,1,0:T(8,128)(2,1)S(1)} all-gather(bf16[1,128,512]{2,1,0:T(8,128)(2,1)S(1)} %copy-done.18), channel_id=1, replica_groups=mesh['thinker'=4,'seq'=8] {'thinker'}, dimensions={0}, use_global_device_ids=true | all-gather | bytes 655360 | tf_op jit(solution)/shard_map/all_gather | solution.py:145
  61.1 3.8 %collective-permute-start = (bf16[4,128,512]{1,2,0:T(8,128)(2,1)S(1)}, bf16[4,128,512]{1,2,0:T(8,128)(2,1)}, u32[]{:S(2)}, u32[]{:S(2)}) collective-permute-start(bf16[4,128,512]{1,2,0:T(8,128)(2,1)S(1)} %copy.175), channel_id=1, source_target_pairs={{0,1},{1,2},{2,3},{3,4},{4,5},{5,6},{6,7},{8,9},{9,10},{10,11},{11... | collective-permute-start | bytes 1572872 | tf_op jit(solution)/shard_map/ppermute | solution.py:14
  72.9 2.4 %fusion.66 = (bf16[4,256,512]{1,2,0:T(8,128)(2,1)S(1)}, bf16[4,256,512]{1,2,0:T(8,128)(2,1)S(1)}) fusion(s32[]{:T(128)S(6)} %select_n.110, bf16[4,128,512]{1,2,0:T(8,128)(2,1)} %collective-permute-done.1, bf16[4,128,512]{1,2,0:T(8,128)(2,1)S(1)} %copy.179, bf16[4,128,512]{1,2,0:T(8,128)(2,1)} %copy-done.10, bf16[4,128,512]{1,2,0:T(8,128)(2,1)} %collective-permute-done), kind=kLoop, calls=%fused_computation.116 | loop fusion | flops 8388608 | bytes 4194308 | tf_op jit(solution)/shard_map/jit(_roll_dynamic)/concatenate | solution.py:150
  76.3 2.0 fusion.57
  78.3 2.0 fusion.61
  80.2 2.0 fusion.53
  82.2 1.3 copy.169
  85.3 2.1 fusion.73
  87.4 3.0 %fusion.75 = bf16[4,256,128,1]{1,2,3,0:T(8,128)(2,1)} fusion(bf16[128,4,4,128]{0,3,2,1:T(8,128)(2,1)S(1)} %copy.199, f32[4,4,128,256]{2,3,1,0:T(8,128)} %fusion.61), kind=kOutput, calls=%fused_computation.125 | convolution fusion | flops 134742016 | bytes 2883584 | tf_op jit(solution)/shard_map/kgij,ikgd->jkd/dot_general | solution.py:36
  91.0 1.3 copy-done.4
  95.8 1.8 copy.205
  97.6 2.8 %fusion.71 = bf16[4,256,128,1]{1,2,3,0:T(8,128)(2,1)} fusion(bf16[128,4,4,128]{0,3,2,1:T(8,128)(2,1)S(1)} %copy.199, f32[4,4,128,256]{2,3,1,0:T(8,128)} %fusion.53), kind=kOutput, calls=%fused_computation.121 | convolution fusion | flops 134742016 | bytes 2883584 | tf_op jit(solution)/shard_map/kgij,ikgd->jkd/dot_general | solution.py:36
  100.4 1.8 copy.216
  102.2 2.2 fusion.51
  106.6 1.8 copy.207
  108.4 4.3 %fusion.45 = (bf16[4,256,512]{2,1,0:T(8,128)(2,1)}, bf16[4,256,512]{2,1,0:T(8,128)(2,1)}) fusion(s32[]{:T(128)S(6)} %select_n.114, bf16[1,256,512]{2,1,0:T(8,128)(2,1)S(1)} %broadcast.197, bf16[1,256,512]{2,1,0:T(8,128)(2,1)S(1)} %copy.214, bf16[1,256,512]{2,1,0:T(8,128)(2,1)S(1)} %copy.215, bf16[1,256,512]{2,1,0:T(8,128)(2,1)} %copy.216, ...), kind=kLoop, calls=%fused_computation.75 | loop fusion | flops 7340032 | bytes 3932164 | tf_op jit(solution)/shard_map/convert_element_type | solution.py:187
  114.2 2.6 %convolution_multiply_fusion.1 = f32[4,128,4,128]{3,1,2,0:T(8,128)} fusion(bf16[256,4,128,1]{0,2,3,1:T(8,128)(2,1)S(1)} %bitcast.378, bf16[4,4,128,256]{2,3,1,0:T(8,128)(2,1)} %copy-done.1), kind=kOutput, calls=%fused_computation.107 | convolution fusion | flops 134479872 | bytes 2359296 | tf_op jit(solution)/shard_map/kgij,jkd->ikgd/dot_general | solution.py:44
  116.8 2.5 %copy.192 = f32[128,2048]{1,0:T(8,128)} copy(f32[128,2048]{0,1:T(8,128)} %bitcast.365) | data formatting | bytes 2097152 | tf_op jit(solution)/shard_map/reshape | solution.py:49
  119.3 1.3 convolution_multiply_fusion.2
  120.6 2.7 %copy.186 = f32[128,2048]{1,0:T(8,128)} copy(f32[128,2048]{0,1:T(8,128)} %bitcast.366) | data formatting | bytes 2097152 | tf_op jit(solution)/shard_map/reshape | solution.py:49
  123.3 1.3 convolution_multiply_fusion
  124.6 2.5 %copy.198 = f32[128,2048]{1,0:T(8,128)} copy(f32[128,2048]{0,1:T(8,128)} %bitcast.367) | data formatting | bytes 2097152 | tf_op jit(solution)/shard_map/reshape | solution.py:49
  127.3 1.6 broadcast_in_dim.111.clone
  128.9 29.2 %while.31 = (s32[]{:T(128)}, bf16[1024,1024]{1,0:T(8,128)(2,1)}, s32[]{:T(128)}, bf16[1024,512]{0,1:T(8,128)(2,1)}, bf16[128,4,4,128]{0,3,2,1:T(8,128)(2,1)S(1)}...) while((s32[]{:T(128)}, bf16[1024,1024]{1,0:T(8,128)(2,1)}, ...), condition=%wide.region_4.0_spmd.clone.clone, body=%wide.region_3.0_spmd.clone.clone.sunk | while | flops 1087047552 | bytes 29587980 | solution.py:132
  130.4 1.3 constant_dynamic-slice_fusion.6
  131.7 2.7 %fusion.156 = f32[4,512,128,4]{2,1,3,0:T(8,128)} fusion(bf16[512,4,128,1]{0,2,3,1:T(8,128)(2,1)S(1)} %bitcast.360, bf16[128,4,4,128]{0,3,2,1:T(8,128)(2,1)S(1)} %get-tuple-element.878), kind=kOutput, calls=%fused_computation.161.clone.1 | convolution fusion | flops 268435456 | bytes 5242880 | tf_op jit(solution)/shard_map/while/body/eval_jaxpr/ikgd,jkd->kgij/dot_general | solution.py:26
  134.4 4.2 %fusion.158 = bf16[4,512,128]{1,2,0:T(8,128)(2,1)S(1)} fusion(bf16[128,4,4,128]{0,3,2,1:T(8,128)(2,1)S(1)} %get-tuple-element.878, f32[4,512,128,4]{2,1,3,0:T(8,128)} %fusion.156, bf16[512,4,128,1]{0,2,3,1:T(8,128)(2,1)S(1)} %bitcast.362, bf16[128,4,4,128]{0,3,2,1:T(8,128)(2,1)S(1)} %get-tuple-element.881, f32[4,4,128]{2,1,0:T(4,128)S(1)} %get-tuple-element.882, ...), kind=kOutput, calls=%fused_computation.19.clone.1 | convolution fusion | flops 543686656 | bytes 6373376 | tf_op jit(solution)/shard_map/while/body/eval_jaxpr/kgij,ikgd->jkd/dot_general | solution.py:40
  138.6 3.2 %fusion.157 = bf16[4,512,128,1]{1,2,3,0:T(8,128)(2,1)S(1)} fusion(bf16[128,4,4,128]{0,3,2,1:T(8,128)(2,1)S(1)} %get-tuple-element.881, f32[4,512,128,4]{2,1,3,0:T(8,128)} %fusion.156, f32[4,4,128]{2,1,0:T(4,128)S(1)} %bitcast.389, pred[128,512]{0,1:T(8,128)(4,1)S(1)} %and_and_fusion.8), kind=kOutput, calls=%fused_computation.11.clone.1 | convolution fusion | flops 272629760 | bytes 5316608 | tf_op jit(solution)/shard_map/while/body/eval_jaxpr/kgij,ikgd->jkd/dot_general | solution.py:36
  146.3 2.7 %fusion.156 = f32[4,512,128,4]{2,1,3,0:T(8,128)} fusion(bf16[512,4,128,1]{0,2,3,1:T(8,128)(2,1)S(1)} %bitcast.360, bf16[128,4,4,128]{0,3,2,1:T(8,128)(2,1)S(1)} %get-tuple-element.878), kind=kOutput, calls=%fused_computation.161.clone.1 | convolution fusion | flops 268435456 | bytes 5242880 | tf_op jit(solution)/shard_map/while/body/eval_jaxpr/ikgd,jkd->kgij/dot_general | solution.py:26
  149.0 4.2 %fusion.158 = bf16[4,512,128]{1,2,0:T(8,128)(2,1)S(1)} fusion(bf16[128,4,4,128]{0,3,2,1:T(8,128)(2,1)S(1)} %get-tuple-element.878, f32[4,512,128,4]{2,1,3,0:T(8,128)} %fusion.156, bf16[512,4,128,1]{0,2,3,1:T(8,128)(2,1)S(1)} %bitcast.362, bf16[128,4,4,128]{0,3,2,1:T(8,128)(2,1)S(1)} %get-tuple-element.881, f32[4,4,128]{2,1,0:T(4,128)S(1)} %get-tuple-element.882, ...), kind=kOutput, calls=%fused_computation.19.clone.1 | convolution fusion | flops 543686656 | bytes 6373376 | tf_op jit(solution)/shard_map/while/body/eval_jaxpr/kgij,ikgd->jkd/dot_general | solution.py:40
  153.2 3.2 %fusion.157 = bf16[4,512,128,1]{1,2,3,0:T(8,128)(2,1)S(1)} fusion(bf16[128,4,4,128]{0,3,2,1:T(8,128)(2,1)S(1)} %get-tuple-element.881, f32[4,512,128,4]{2,1,3,0:T(8,128)} %fusion.156, f32[4,4,128]{2,1,0:T(4,128)S(1)} %bitcast.389, pred[128,512]{0,1:T(8,128)(4,1)S(1)} %and_and_fusion.8), kind=kOutput, calls=%fused_computation.11.clone.1 | convolution fusion | flops 272629760 | bytes 5316608 | tf_op jit(solution)/shard_map/while/body/eval_jaxpr/kgij,ikgd->jkd/dot_general | solution.py:36
  159.4 21.8 %while.32 = (s32[]{:T(128)}, f32[128,2048]{0,1:T(8,128)S(1)}, bf16[1024,512]{0,1:T(8,128)(2,1)}, s32[]{:T(128)}, bf16[128,4,4,128]{3,0,2,1:T(8,128)(2,1)S(1)}, /...) while((s32[]{:T(128)}, f32[128,2048]{0,1:T(8,128)S(1)}, ...), condition=%wide.region_2.3_spmd.clone.clone.clone, body=%wide.region_1.2_spmd.clone.clone.clone.sunk | while | flops 812582784 | bytes 17455584 | solution.py:118
  160.8 2.1 constant_dynamic-slice_fusion.7
  162.9 2.7 %fusion.164 = f32[4,512,128,4]{2,1,3,0:T(8,128)} fusion(bf16[512,4,128,1]{0,2,3,1:T(8,128)(2,1)S(1)} %bitcast.358, bf16[128,4,4,128]{3,0,2,1:T(8,128)(2,1)S(1)} %get-tuple-element.836), kind=kOutput, calls=%fused_computation.162.clone.1 | convolution fusion | flops 268435456 | bytes 5242880 | tf_op jit(solution)/shard_map/while/body/eval_jaxpr/ikgd,jkd->kgij/dot_general | solution.py:26
  165.7 4.3 %fusion.165 = f32[4,128,4,128]{3,1,2,0:T(8,128)S(1)} fusion(bf16[512,4,128,1]{0,2,3,1:T(8,128)(2,1)S(1)} %bitcast.359, f32[4,512,128,4]{2,1,3,0:T(8,128)} %fusion.164, bf16[512,4,128,1]{0,2,3,1:T(8,128)(2,1)} %bitcast.361, bf16[128,4,4,128]{3,0,2,1:T(8,128)(2,1)} %get-tuple-element.839, f32[4,4,128]{2,1,0:T(4,128)S(1)} %get-tuple-element.840, ...), kind=kOutput, calls=%fused_computation.39.clone.1 | convolution fusion | flops 543424512 | bytes 6897664 | tf_op jit(solution)/shard_map/while/body/eval_jaxpr/kgij,jkd->ikgd/dot_general | solution.py:44
  171.6 2.1 constant_dynamic-slice_fusion.7
  173.7 2.7 %fusion.164 = f32[4,512,128,4]{2,1,3,0:T(8,128)} fusion(bf16[512,4,128,1]{0,2,3,1:T(8,128)(2,1)S(1)} %bitcast.358, bf16[128,4,4,128]{3,0,2,1:T(8,128)(2,1)S(1)} %get-tuple-element.836), kind=kOutput, calls=%fused_computation.162.clone.1 | convolution fusion | flops 268435456 | bytes 5242880 | tf_op jit(solution)/shard_map/while/body/eval_jaxpr/ikgd,jkd->kgij/dot_general | solution.py:26
  176.4 4.5 %fusion.165 = f32[4,128,4,128]{3,1,2,0:T(8,128)S(1)} fusion(bf16[512,4,128,1]{0,2,3,1:T(8,128)(2,1)S(1)} %bitcast.359, f32[4,512,128,4]{2,1,3,0:T(8,128)} %fusion.164, bf16[512,4,128,1]{0,2,3,1:T(8,128)(2,1)} %bitcast.361, bf16[128,4,4,128]{3,0,2,1:T(8,128)(2,1)} %get-tuple-element.839, f32[4,4,128]{2,1,0:T(4,128)S(1)} %get-tuple-element.840, ...), kind=kOutput, calls=%fused_computation.39.clone.1 | convolution fusion | flops 543424512 | bytes 6897664 | tf_op jit(solution)/shard_map/while/body/eval_jaxpr/kgij,jkd->ikgd/dot_general | solution.py:44
  181.2 1.3 copy.185
  183.5 1.9 collective-permute-start.3
  186.4 3.0 %collective-permute-start.2 = (bf16[128,512]{1,0:T(8,128)(2,1)S(1)}, bf16[128,512]{1,0:T(8,128)(2,1)S(1)}, u32[]{:S(2)}, u32[]{:S(2)}) collective-permute-start(bf16[128,512]{1,0:T(8,128)(2,1)S(1)} %slice_bitcast_fusion.2), channel_id=1, source_target_pairs={{1,0},{2,1},{3,2},{4,3},{5,4},{6,5},{7,6},{9,8},{10,9},{11,10},{12... | collective-permute-start | bytes 393224 | tf_op jit(solution)/shard_map/ppermute | solution.py:14
  189.4 2.6 %fusion.77 = bf16[1,128,2048]{2,1,0:T(8,128)(2,1)} fusion(f32[128,2048]{1,0:T(8,128)} %copy.198, f32[128,2048]{1,0:T(8,128)S(1)} %copy-done.8, f32[128,2048]{1,0:T(8,128)} %copy.185, f32[128,2048]{1,0:T(8,128)S(1)} %copy-done.9), kind=kLoop, calls=%fused_computation.129 | loop fusion | flops 1048576 | bytes 4718592 | tf_op jit(solution)/shard_map/broadcast_in_dim | solution.py:196
  192.0 19.8 %reduce-scatter.4.cloned.1.call-done = bf16[128,1024]{1,0:T(8,128)(2,1)} async-done(((bf16[1024,1024]{1,0:T(8,128)(2,1)}), bf16[128,1024]{1,0:T(8,128)(2,1)}) %reduce-scatter.4.cloned.1.call-update) | async-done | bytes 262160 | tf_op jit(solution)/shard_map/reduce_scatter | solution.py:131
  (141 shorter events, 33.0 us)
Async XLA Ops:
  8.0 38.4 %copy-start.18 = (bf16[1,128,512]{2,1,0:T(8,128)(2,1)S(1)}, bf16[1,128,512]{2,1,0:T(8,128)(2,1)}, u32[]{:S(2)}) copy-start(bf16[1,128,512]{2,1,0:T(8,128)(2,1)} %param.17) | copy-start | bytes 393220
  8.0 10.3 %copy-start.19 = (bf16[1,128,512]{2,1,0:T(8,128)(2,1)S(1)}, bf16[1,128,512]{2,1,0:T(8,128)(2,1)}, u32[]{:S(2)}) copy-start(bf16[1,128,512]{2,1,0:T(8,128)(2,1)} %param.18) | copy-start | bytes 393220
  8.0 119.2 %all-gather.3.cloned.1.call-start = ((), (), s32[]{:S(2)}) async-start(), calls=%async_computation.4 | async-start | bytes 1179648 | tf_op jit(solution)/shard_map/all_gather | solution.py:105
  11.8 70.4 %all-to-all-start = ((bf16[32,4,1,2048]{3,1,2,0:T(4,128)(2,1)}), bf16[32,4,1,2048]{3,1,2,0:T(4,128)(2,1)}, u32[]{:S(2)}, u32[]{:S(2)}) async-start(bf16[32,4,1,2048]{3,1,2,0:T(4,128)(2,1)} %reshape.154), calls=%async_computation | async-start | bytes 1048576 | tf_op jit(solution)/shard_map/all_to_all | solution.py:72
  18.2 47.6 %copy-start.25 = (s32[1,3,1]{1,2,0:T(1,128)S(1)}, s32[1,3,1]{1,2,0:T(1,128)}, u32[]{:S(2)}) copy-start(s32[1,3,1]{1,2,0:T(1,128)} %param.23) | copy-start | bytes 40
  18.2 50.0 %copy-start.20 = (bf16[1,128,2048]{2,1,0:T(8,128)(2,1)S(1)}, bf16[1,128,2048]{2,1,0:T(8,128)(2,1)}, u32[]{:S(2)}) copy-start(bf16[1,128,2048]{2,1,0:T(8,128)(2,1)} %param.16) | copy-start | bytes 1572868
  18.2 109.0 %all-gather.5.cloned.1.call-start = ((), (), s32[]{:S(2)}) async-start(), calls=%async_computation.5 | async-start | bytes 1179648 | tf_op jit(solution)/shard_map/all_gather | solution.py:106
  39.8 28.7 %copy-start.21 = (bf16[1,128,2048]{2,1,0:T(8,128)(2,1)S(1)}, bf16[1,128,2048]{2,1,0:T(8,128)(2,1)}, u32[]{:S(2)}) copy-start(bf16[1,128,2048]{2,1,0:T(8,128)(2,1)} %param.19) | copy-start | bytes 1572868
  40.1 32.8 %collective-permute-start.1 = (bf16[4,128,512]{1,2,0:T(8,128)(2,1)S(1)}, bf16[4,128,512]{1,2,0:T(8,128)(2,1)}, u32[]{:S(2)}, u32[]{:S(2)}) collective-permute-start(bf16[4,128,512]{1,2,0:T(8,128)(2,1)S(1)} %copy.179), channel_id=1, source_target_pairs={{0,1},{1,2},{2,3},{3,4},{4,5},{5,6},{6,7},{8,9},{9,10},{10,11},{11... | collective-permute-start | bytes 1572872 | tf_op jit(solution)/shard_map/ppermute | solution.py:14
  61.1 8.3 %copy-start.10 = (bf16[4,128,512]{1,2,0:T(8,128)(2,1)}, bf16[4,128,512]{1,2,0:T(8,128)(2,1)S(1)}, u32[]{:S(2)}) copy-start(bf16[4,128,512]{1,2,0:T(8,128)(2,1)S(1)} %copy.175) | copy-start | bytes 1572868
  61.1 8.3 %copy-start.24 = (s32[4]{0:T(128)S(1)}, s32[4]{0:T(128)}, u32[]{:S(2)}) copy-start(s32[4]{0:T(128)} %param.22) | copy-start | bytes 52
  61.1 11.8 %collective-permute-start = (bf16[4,128,512]{1,2,0:T(8,128)(2,1)S(1)}, bf16[4,128,512]{1,2,0:T(8,128)(2,1)}, u32[]{:S(2)}, u32[]{:S(2)}) collective-permute-start(bf16[4,128,512]{1,2,0:T(8,128)(2,1)S(1)} %copy.175), channel_id=1, source_target_pairs={{0,1},{1,2},{2,3},{3,4},{4,5},{5,6},{6,7},{8,9},{9,10},{10,11},{11... | collective-permute-start | bytes 1572872 | tf_op jit(solution)/shard_map/ppermute | solution.py:14
  65.7 116.9 %reduce-scatter.8.cloned.1.call-start = ((), (), s32[]{:S(2)}) async-start(), calls=%async_computation.8 | async-start | bytes 1310720 | tf_op jit(solution)/shard_map/reduce_scatter | solution.py:186
  75.3 0.9 copy-start.26
  76.2 4.0 %copy-start.13 = (bf16[1,256,512]{1,2,0:T(8,128)(2,1)}, bf16[1,256,512]{1,2,0:T(8,128)(2,1)S(1)}, u32[]{:S(2)}) copy-start(bf16[1,256,512]{1,2,0:T(8,128)(2,1)S(1)} %get-tuple-element.649) | copy-start | bytes 786436
  76.2 4.0 %copy-start.15 = (bf16[1,256,512]{1,2,0:T(8,128)(2,1)}, bf16[1,256,512]{1,2,0:T(8,128)(2,1)S(1)}, u32[]{:S(2)}) copy-start(bf16[1,256,512]{1,2,0:T(8,128)(2,1)S(1)} %get-tuple-element.650) | copy-start | bytes 786436
  76.2 4.0 %copy-start.11 = (bf16[1,256,512]{1,2,0:T(8,128)(2,1)}, bf16[1,256,512]{1,2,0:T(8,128)(2,1)S(1)}, u32[]{:S(2)}) copy-start(bf16[1,256,512]{1,2,0:T(8,128)(2,1)S(1)} %get-tuple-element.651) | copy-start | bytes 786436
  87.4 3.0 %copy-start.5 = (f32[4,4,128,256]{2,3,1,0:T(8,128)S(1)}, f32[4,4,128,256]{2,3,1,0:T(8,128)}, u32[]{:S(2)}) copy-start(f32[4,4,128,256]{2,3,1,0:T(8,128)} %fusion.57) | copy-start | bytes 6291460
  87.4 3.0 %copy-start.17 = (bf16[1,256,512]{1,2,0:T(8,128)(2,1)S(1)}, bf16[1,256,512]{1,2,0:T(8,128)(2,1)}, u32[]{:S(2)}) copy-start(bf16[1,256,512]{1,2,0:T(8,128)(2,1)} %get-tuple-element.647) | copy-start | bytes 786436
  90.4 1.8 copy-start.4
  91.0 2.3 %copy-start.1 = (bf16[4,4,128,256]{2,3,1,0:T(8,128)(2,1)}, bf16[4,4,128,256]{2,3,1,0:T(8,128)(2,1)S(1)}, u32[]{:S(2)}) copy-start(bf16[4,4,128,256]{2,3,1,0:T(8,128)(2,1)S(1)} %fusion.55) | copy-start | bytes 3145732
  104.4 1.0 copy-start.2
  112.7 1.5 copy-start.16
  112.7 72.7 %reduce-scatter.6.cloned.1.call-start = ((), (), s32[]{:S(2)}) async-start(), calls=%async_computation.7 | async-start | bytes 1310720 | tf_op jit(solution)/shard_map/reduce_scatter | solution.py:183
  114.2 5.1 %copy-start.14 = (bf16[1,256,512]{1,2,0:T(8,128)(2,1)S(1)}, bf16[1,256,512]{1,2,0:T(8,128)(2,1)}, u32[]{:S(2)}) copy-start(bf16[1,256,512]{1,2,0:T(8,128)(2,1)} %copy-done.13) | copy-start | bytes 786436
  119.3 4.0 %copy-start.12 = (bf16[1,256,512]{1,2,0:T(8,128)(2,1)S(1)}, bf16[1,256,512]{1,2,0:T(8,128)(2,1)}, u32[]{:S(2)}) copy-start(bf16[1,256,512]{1,2,0:T(8,128)(2,1)} %copy-done.11) | copy-start | bytes 786436
  120.6 2.7 %copy-start.3 = (bf16[4,4,128,256]{2,3,1,0:T(8,128)(2,1)S(1)}, bf16[4,4,128,256]{2,3,1,0:T(8,128)(2,1)}, u32[]{:S(2)}) copy-start(bf16[4,4,128,256]{2,3,1,0:T(8,128)(2,1)} %copy-done.2) | copy-start | bytes 3145732
  127.2 84.6 %reduce-scatter.4.cloned.1.call-start = ((), (), s32[]{:S(2)}) async-start(), calls=%async_computation.6 | async-start | bytes 2359296 | tf_op jit(solution)/shard_map/reduce_scatter | solution.py:131
  128.9 9.6 %copy-start.6 = (bf16[128,4,4,128]{0,3,2,1:T(8,128)(2,1)}, bf16[128,4,4,128]{0,3,2,1:T(8,128)(2,1)S(1)}, u32[]{:S(2)}) copy-start(bf16[128,4,4,128]{0,3,2,1:T(8,128)(2,1)S(1)} %get-tuple-element.881) | copy-start | bytes 1572868 | tf_op jit(solution)/shard_map/while
  142.3 1.2 copy-start.7
  143.5 9.6 %copy-start.6 = (bf16[128,4,4,128]{0,3,2,1:T(8,128)(2,1)}, bf16[128,4,4,128]{0,3,2,1:T(8,128)(2,1)S(1)}, u32[]{:S(2)}) copy-start(bf16[128,4,4,128]{0,3,2,1:T(8,128)(2,1)S(1)} %get-tuple-element.881) | copy-start | bytes 1572868 | tf_op jit(solution)/shard_map/while
  157.0 1.2 copy-start.7
  158.2 1.2 copy-start
  181.2 8.2 %copy-start.8 = (f32[128,2048]{1,0:T(8,128)S(1)}, f32[128,2048]{1,0:T(8,128)}, u32[]{:S(2)}) copy-start(f32[128,2048]{1,0:T(8,128)} %copy.192) | copy-start | bytes 3145732
  181.2 8.2 %copy-start.9 = (f32[128,2048]{1,0:T(8,128)S(1)}, f32[128,2048]{1,0:T(8,128)}, u32[]{:S(2)}) copy-start(f32[128,2048]{1,0:T(8,128)} %copy.186) | copy-start | bytes 3145732
  183.5 29.3 %collective-permute-start.3 = (bf16[128,512]{1,0:T(8,128)(2,1)S(1)}, bf16[128,512]{1,0:T(8,128)(2,1)S(1)}, u32[]{:S(2)}, u32[]{:S(2)}) collective-permute-start(bf16[128,512]{1,0:T(8,128)(2,1)S(1)} %slice_bitcast_fusion), channel_id=1, source_target_pairs={{1,0},{2,1},{3,2},{4,3},{5,4},{6,5},{7,6},{9,8},{10,9},{11,10},{12... | collective-permute-start | bytes 393224 | tf_op jit(solution)/shard_map/ppermute | solution.py:14
  186.3 26.5 %copy-start.22 = (bf16[1,256,512]{2,1,0:T(8,128)(2,1)S(1)}, bf16[1,256,512]{2,1,0:T(8,128)(2,1)}, u32[]{:S(2)}) copy-start(bf16[1,256,512]{2,1,0:T(8,128)(2,1)} %reduce-scatter.8.cloned.1.call-done) | copy-start | bytes 786436
  186.4 26.5 %copy-start.23 = (bf16[1,256,512]{2,1,0:T(8,128)(2,1)S(1)}, bf16[1,256,512]{2,1,0:T(8,128)(2,1)}, u32[]{:S(2)}) copy-start(bf16[1,256,512]{2,1,0:T(8,128)(2,1)} %reduce-scatter.6.cloned.1.call-done) | copy-start | bytes 786436
  186.4 26.4 %collective-permute-start.2 = (bf16[128,512]{1,0:T(8,128)(2,1)S(1)}, bf16[128,512]{1,0:T(8,128)(2,1)S(1)}, u32[]{:S(2)}, u32[]{:S(2)}) collective-permute-start(bf16[128,512]{1,0:T(8,128)(2,1)S(1)} %slice_bitcast_fusion.2), channel_id=1, source_target_pairs={{1,0},{2,1},{3,2},{4,3},{5,4},{6,5},{7,6},{9,8},{10,9},{11,10},{12... | collective-permute-start | bytes 393224 | tf_op jit(solution)/shard_map/ppermute | solution.py:14
Sparse Core Ops, SparseCore 0:
  11.3 27.3 all-gather.2
  65.8 23.7 all-gather.4
Sparse Core Ops, SparseCore 1:
  112.8 24.9 reduce-scatter.7
  140.0 25.7 reduce-scatter.5
  168.9 42.8 reduce-scatter.3
where the time goes:
time: 224 us; the launch traced here: 221 us
  matrix products  59.4 us (27%)
  local copies, waits for them, and re-layouts  44.8 us (20%)
  blocking collectives  35.8 us (16%)
  starting transfers between devices  21.9 us (10%)
  other arithmetic  21 us (9%)
  waiting for transfers between devices  19.9 us (9%)
  between operations  18.1 us (8%)
    all_gather x1, blocking collectives, shards(): lax.all_gather(values, 'thinker', axis=0, tiled=True)  21.5 us
    reduce_scatter x1, waiting for transfers between devices, shards(): lax.psum_scatter(lax.fori_loop(0, rows * lax.axis_size('seq') // sub_rows...  19.8 us
    dot_general x7, matrix products, pair_grads(): jnp.einsum('ikgd,jkd->kgij', query_heads, key_heads, preferred_element_ty...  16.8 us
    ppermute x4, starting transfers between devices, from_behind(): return lax.ppermute(block, axis, route)  15.1 us
    all_gather x1, blocking collectives, shards(): lax.all_gather(keys, 'thinker', axis=0, tiled=True)  14.3 us
    dot_general x5, matrix products, pair_grads(): jnp.einsum('kgij,ikgd->jkd', probs_low, upstream_heads, preferred_element...  14.2 us
    dot_general x5, matrix products, pair_grads(): jnp.einsum('kgij,jkd->ikgd', dscores_low, key_heads, preferred_element_ty...  14 us
    dot_general x5, matrix products, pair_grads(): jnp.einsum('kgij,ikgd->jkd', dscores_low, query_heads, preferred_element_...  11.1 us
  transfers between devices with their start and end apart: 10, of which 1 were waited for; matrix products, arithmetic and copies ran while one was open for 54% of the time, Pallas kernels for 0%

commit v1 on v0

v1 whole, which is shorter than its diff:
```python
import functools
import math

import jax
import jax.numpy as jnp
from jax import lax
from jax.experimental import pallas as pl
from jax.experimental.pallas import tpu as pltpu
from jax.sharding import PartitionSpec as P

BLOCK = 128
MESH = pl.DeviceIdType.MESH
F32 = jnp.float32
BF16 = jnp.bfloat16
FAR = 1e30


def dot_tt(a, b):
    return lax.dot_general(a, b, (((1,), (1,)), ((), ())), preferred_element_type=F32)


def dot_nn(a, b):
    return lax.dot_general(a, b, (((1,), (0,)), ((), ())), preferred_element_type=F32)


def dot_t(a, b):
    return lax.dot_general(a, b, (((0,), (0,)), ((), ())), preferred_element_type=F32)


def body(
    T, S, G, KV, HD,
    lengths, mask, q_ref, k_ref, v_ref, o_ref, lse_ref, up_ref,
    dq_ref, dk_ref, dv_ref,
    rows_in, kvall, sibc, sibp, gpart, gown, gsp, gspr, gsc, gz, gzr,
    qs, dos, lse2, delta, dqa, acc,
    up_send, up_recv, kv_send, kv_recv, z_send, z_recv, h_send, h_recv,
    g_send, g_recv, b_send, b_recv, y_send, y_recv,
):
    N = T * S
    ROWS = 128
    W = up_ref.shape[1]
    C = (KV * G * HD) // W
    shift = int(math.log2(N))
    GQ = G * ROWS
    factor = HD ** (-0.5)
    log2e = math.log2(math.e)
    t = lax.axis_index("thinker")
    s = lax.axis_index("seq")
    me = t * S + s

    def place(d):
        return (d // S, d % S)

    barrier = pltpu.get_barrier_semaphore()

    def greet(i, c):
        pl.semaphore_signal(
            barrier, inc=1, device_id=place(lax.rem(me + i, N)), device_id_type=MESH
        )
        return c

    lax.fori_loop(1, N, greet, 0)

    for g in range(KV):
        kvall[s, g] = k_ref[:, g * HD:(g + 1) * HD]
        kvall[s, KV + g] = v_ref[:, g * HD:(g + 1) * HD]

    pl.semaphore_wait(barrier, N - 1)

    def remote(src, dst, ss, rs, where):
        return pltpu.make_async_remote_copy(
            src_ref=src, dst_ref=dst, send_sem=ss, recv_sem=rs,
            device_id=where, device_id_type=MESH,
        )

    def send_up(i, c):
        d = lax.rem(me + i, N)
        remote(
            up_ref.at[pl.ds(pl.multiple_of(d * 16, 16), 16)],
            rows_in.at[pl.ds(pl.multiple_of(me * 16, 16), 16)],
            up_send, up_recv, place(d),
        ).start()
        return c

    lax.fori_loop(1, N, send_up, 0)

    def z_copy(o):
        return remote(
            kvall.at[s], sibc.at[o - 1], z_send.at[o - 1], z_recv.at[o - 1],
            (lax.rem(t + T - o, T), s),
        )

    for o in range(1, T):
        z_copy(o).start()

    def kv_copy(d):
        return remote(kvall.at[s], kvall.at[s], kv_send.at[d], kv_recv.at[s], (t, d))

    def kv_start(d, c):
        kv_copy(d).start()
        return c

    lax.fori_loop(s + 1, S, kv_start, 0)

    rows_in[pl.ds(pl.multiple_of(me * 16, 16), 16), :] = up_ref[
        pl.ds(pl.multiple_of(me * 16, 16), 16), :
    ]
    mine = lengths[t]
    first = s * ROWS
    lane = lax.broadcasted_iota(jnp.int32, (1, GQ), 1) & (ROWS - 1)
    live = (first + lane) < mine
    for g in range(KV):
        qs[g] = jnp.concatenate(
            [q_ref[:, (g * G + i) * HD:(g * G + i + 1) * HD] for i in range(G)], axis=0
        )
        row = jnp.concatenate([lse_ref[g * G + i:g * G + i + 1, :] for i in range(G)], axis=1)
        lse2[g] = jnp.where(live, row * log2e, FAR)
    dqa[...] = jnp.zeros_like(dqa)

    @pl.when(s == 0)
    def _():
        sibp[...] = jnp.zeros_like(sibp)

    whole = rows_in.at[pl.ds(0, (N - 1) * 16)]
    pltpu.make_async_copy(whole, whole, up_recv).wait()
    pos = lax.broadcasted_iota(jnp.int32, (ROWS, N * 16), 0)
    col = lax.broadcasted_iota(jnp.int32, (ROWS, N * 16), 1)
    base = (pos & (N - 1)) * 16 + lax.shift_right_logical(pos, shift) * C
    arrived = rows_in[...]
    per = W // HD
    for c in range(C):
        pick = jnp.where(col == base + c, 1.0, 0.0).astype(BF16)
        part = dot_nn(pick, arrived).astype(BF16)
        for i in range(per):
            h = c * per + i
            dos[h // G, (h % G) * ROWS:(h % G + 1) * ROWS, :] = part[:, i * HD:(i + 1) * HD]
    ones = jnp.ones((8, HD), BF16)
    for g in range(KV):
        og = jnp.concatenate(
            [o_ref[:, (g * G + i) * HD:(g * G + i + 1) * HD] for i in range(G)], axis=0
        )
        prod = dos[g].astype(F32) * og.astype(F32)
        high = prod.astype(BF16)
        low = (prod - high.astype(F32)).astype(BF16)
        delta[g] = (dot_tt(ones, high) + dot_tt(ones, low))[0:1, :]

    key_i = lax.broadcasted_iota(jnp.int32, (ROWS, GQ), 0)
    qry_i = lax.broadcasted_iota(jnp.int32, (ROWS, GQ), 1) & (ROWS - 1)
    scale = factor * log2e

    def own(b, diagonal):
        def step(g, c):
            km = kvall[b, g]
            vm = kvall[b, KV + g]
            qg = qs[g]
            dg = dos[g]
            p = jnp.exp2(dot_tt(km, qg) * scale - lse2[g])
            if diagonal:
                p = jnp.where(key_i <= qry_i, p, 0.0)
            ds = p * (dot_tt(vm, dg) - delta[g])
            pb = p.astype(BF16)
            db = ds.astype(BF16)
            dv = dot_nn(pb, dg)
            dk = dot_nn(db, qg) * factor
            if diagonal:
                acc[g] = dk
                acc[KV + g] = dv
            else:
                gpart[b, g] = dk.astype(BF16)
                gpart[b, KV + g] = dv.astype(BF16)
            dqa[g] += dot_t(db, km)
            return c

        lax.fori_loop(0, KV, step, 0)

    own(s, True)

    def shift_copy(o):
        return remote(
            sibc.at[o - 1], sibp.at[o - 1], h_send.at[o - 1], h_recv.at[o - 1],
            (t, lax.rem(s + 1, S)),
        )

    def back_copy(o):
        return remote(
            gsp.at[o - 1], gspr.at[o - 1], b_send.at[o - 1], b_recv.at[o - 1],
            (t, lax.rem(s + S - 1, S)),
        )

    for o in range(1, T):
        z_copy(o).wait_recv()

        @pl.when(s < S - 1)
        def _():
            shift_copy(o).start()

    for o in range(1, T):
        @pl.when(s > 0)
        def _():
            shift_copy(o).wait_recv()

        other = lengths[lax.rem(t + o, T)]
        edge = jnp.where(mask[o - 1] == 1, other - first, -2 * ROWS)

        def step(g, c):
            kc = sibc[o - 1, g]
            vc = sibc[o - 1, KV + g]
            kp = sibp[o - 1, g]
            vp = sibp[o - 1, KV + g]
            qg = qs[g]
            dg = dos[g]
            near = key_i <= qry_i
            place_k = jnp.where(near, key_i, key_i - ROWS)
            keep = (place_k < edge) & (place_k >= -first)
            st = jnp.where(near, dot_tt(kc, qg), dot_tt(kp, qg))
            p = jnp.where(keep, jnp.exp2(st * scale - lse2[g]), 0.0)
            dp = jnp.where(near, dot_tt(vc, dg), dot_tt(vp, dg))
            ds = p * (dp - delta[g])
            pc = jnp.where(near, p, 0.0).astype(BF16)
            pp = jnp.where(near, 0.0, p).astype(BF16)
            dc = jnp.where(near, ds, 0.0).astype(BF16)
            de = jnp.where(near, 0.0, ds).astype(BF16)
            gsc[o - 1, g] = dot_nn(dc, qg) * factor
            gsc[o - 1, KV + g] = dot_nn(pc, dg)
            gsp[o - 1, g] = (dot_nn(de, qg) * factor).astype(BF16)
            gsp[o - 1, KV + g] = dot_nn(pp, dg).astype(BF16)
            dqa[g] += dot_t(dc, kc) + dot_t(de, kp)
            return c

        lax.fori_loop(0, KV, step, 0)

        @pl.when(s > 0)
        def _():
            back_copy(o).start()

    def g_copy(b):
        return remote(gpart.at[b], gown.at[s], g_send.at[b], g_recv.at[s], (t, b))

    def kv_arrival(b):
        return remote(kvall.at[b], kvall.at[b], kv_send.at[b], kv_recv.at[b], (t, b))

    def own_step(b, c):
        kv_arrival(b).wait_recv()
        own(b, False)
        g_copy(b).start()
        return c

    half = s // 2
    lax.fori_loop(0, half, own_step, 0)

    def y_copy(o):
        return remote(
            gz.at[o - 1], gzr.at[o - 1], y_send.at[o - 1], y_recv.at[o - 1],
            (lax.rem(t + o, T), s),
        )

    for o in range(1, T):
        @pl.when(s < S - 1)
        def _():
            back_copy(o).wait_recv()
            gz[o - 1] = (gsc[o - 1] + gspr[o - 1].astype(F32)).astype(BF16)

        @pl.when(s == S - 1)
        def _():
            gz[o - 1] = gsc[o - 1].astype(BF16)

        y_copy(o).start()

    lax.fori_loop(half, s, own_step, 0)

    for g in range(KV):
        for i in range(G):
            h = g * G + i
            dq_ref[:, h * HD:(h + 1) * HD] = (
                dqa[g, i * ROWS:(i + 1) * ROWS, :] * factor
            ).astype(BF16)

    def g_arrival(b, c):
        remote(gpart.at[b], gown.at[b], g_send.at[b], g_recv.at[b], (t, b)).wait_recv()
        acc[...] += gown[b].astype(F32)
        return c

    lax.fori_loop(s + 1, S, g_arrival, 0)
    for o in range(1, T):
        y_copy(o).wait_recv()
        acc[...] += gzr[o - 1].astype(F32)
    for g in range(KV):
        dk_ref[:, g * HD:(g + 1) * HD] = acc[g].astype(BF16)
        dv_ref[:, g * HD:(g + 1) * HD] = acc[KV + g].astype(BF16)

    sent = up_ref.at[pl.ds(0, (N - 1) * 16)]
    pltpu.make_async_copy(sent, sent, up_send).wait()

    def kv_left(d, c):
        kv_copy(d).wait_send()
        return c

    lax.fori_loop(s + 1, S, kv_left, 0)

    def g_left(b, c):
        g_copy(b).wait_send()
        return c

    lax.fori_loop(0, s, g_left, 0)
    for o in range(1, T):
        z_copy(o).wait_send()
        y_copy(o).wait_send()

        @pl.when(s < S - 1)
        def _():
            shift_copy(o).wait_send()

        @pl.when(s > 0)
        def _():
            back_copy(o).wait_send()


def shards(queries, keys, values, forward_out, logsumexp, upstream, lengths, sibling_mask):
    T = lax.axis_size("thinker")
    S = lax.axis_size("seq")
    N = T * S
    rows, qw = queries.shape[1:]
    kw = keys.shape[2]
    heads = logsumexp.shape[1]
    HD = qw // heads
    KV = kw // HD
    G = heads // KV
    width = (rows // N) * qw // 16
    up = upstream.reshape(N * 16, width)
    block = (2 * KV, rows, HD)
    vmem = pl.BlockSpec(memory_space=pltpu.VMEM)
    smem = pl.BlockSpec(memory_space=pltpu.SMEM)
    dma = pltpu.SemaphoreType.DMA
    dq, dk, dv = pl.pallas_call(
        functools.partial(body, T, S, G, KV, HD),
        out_shape=(
            jax.ShapeDtypeStruct((rows, qw), BF16),
            jax.ShapeDtypeStruct((rows, kw), BF16),
            jax.ShapeDtypeStruct((rows, kw), BF16),
        ),
        in_specs=[smem, smem] + [vmem] * 6,
        out_specs=(vmem, vmem, vmem),
        scratch_shapes=[
            pltpu.VMEM((N * 16, width), BF16),
            pltpu.VMEM((S,) + block, BF16),
            pltpu.VMEM((T - 1,) + block, BF16),
            pltpu.VMEM((T - 1,) + block, BF16),
            pltpu.VMEM((S,) + block, BF16),
            pltpu.VMEM((S,) + block, BF16),
            pltpu.VMEM((T - 1,) + block, BF16),
            pltpu.VMEM((T - 1,) + block, BF16),
            pltpu.VMEM((T - 1,) + block, F32),
            pltpu.VMEM((T - 1,) + block, BF16),
            pltpu.VMEM((T - 1,) + block, BF16),
            pltpu.VMEM((KV, G * rows, HD), BF16),
            pltpu.VMEM((KV, G * rows, HD), BF16),
            pltpu.VMEM((KV, 1, G * rows), F32),
            pltpu.VMEM((KV, 1, G * rows), F32),
            pltpu.VMEM((KV, G * rows, HD), F32),
            pltpu.VMEM(block, F32),
            dma, dma, dma((S,)), dma((S,)), dma((T - 1,)), dma((T - 1,)),
            dma((T - 1,)), dma((T - 1,)), dma((S,)), dma((S,)),
            dma((T - 1,)), dma((T - 1,)), dma((T - 1,)), dma((T - 1,)),
        ],
        compiler_params=pltpu.CompilerParams(
            collective_id=0, has_side_effects=True, vmem_limit_bytes=52 * 1024 * 1024
        ),
    )(
        lengths, sibling_mask.reshape(-1), queries[0], keys[0], values[0],
        forward_out[0], logsumexp[0], up,
    )
    return dq[None], dk[None], dv[None]


def solution(mesh):
    placed = (
        P("thinker", "seq", None),
        P("thinker", "seq", None),
        P("thinker", "seq", None),
        P("thinker", "seq", None),
        P("thinker", None, "seq"),
        P(None, ("thinker", "seq"), None),
        P(),
        P("thinker", None, "seq"),
    )
    return jax.shard_map(
        shards,
        mesh=mesh,
        in_specs=placed,
        out_specs=(P("thinker", "seq", None), P("thinker", "seq", None), P("thinker", "seq", None)),
        check_vma=False,
    )
```

time: 224 us -> 87.7 us (0.39)
  the two profiles are of different devices: /device:TPU:11 before, /device:TPU:3 now
where the time goes in v1:
time: 87.7 us; the launch traced here: 87.6 us
  Pallas kernels  82.5 us (94%)
  local copies, waits for them, and re-layouts  4.34 us (5%)
    pallas_call x1, Pallas kernels, shards(): pl.pallas_call(functools.partial(body, T, S, G, KV, HD), out_shape=(jax.S...  82.5 us
    reshape x1, local copies, waits for them, and re-layouts, shards(): up = upstream.reshape(N * 16, width)  2.21 us
    unnamed x15, local copies, waits for them, and re-layouts  2.13 us

profile of v1, /device:TPU:3, one launch (start us, length us, event | category | flops | bytes accessed | tf_op | source)
XLA Modules:
  0.0 87.6 jit_solution(4391869439676889960)
XLA Ops:
  0.6 0.0 copy-start
  0.6 0.0 copy-start.1
  0.7 0.0 copy-start.2
  0.7 0.0 copy-start.3
  0.7 0.0 copy-start.4
  0.7 0.0 copy-start.5
  0.7 2.2 %reshape.13.up_ref = bf16[512,512]{1,0:T(8,128)(2,1)} reshape(bf16[128,1,2048]{2,0,1:T(8,128)(2,1)} %param.13) | data formatting | bytes 1048576 | tf_op jit(solution)/shard_map/reshape | solution.py:329
  2.9 0.0 copy-done
  2.9 0.0 copy-done.1
  2.9 0.0 copy-done.2
  2.9 0.0 copy-done.3
  2.9 0.0 copy-done.4
  2.9 0.0 copy-done.5
  2.9 82.5 %shard_map.103 = (bf16[128,2048]{1,0:T(8,128)(2,1)S(1)}, bf16[128,512]{1,0:T(8,128)(2,1)S(1)}, bf16[128,512]{1,0:T(8,128)(2,1)S(1)}) custom-call(s32[4]{0:T(128)S(1)} %copy-done.4, s32[3]{0:T(128)S(1)} %bitcast.18, bf16[128,2048]{1,0:T(8,128)(2,1)S(1)} %bitcast.11, bf16[128,512]{1,0:T(8,128)(2,1)S(1)} %bitcast.13, bf16[128,512]{1,0:T(8,128)(2,1)S(1)} %bitcast.14, ...), custom_call_target="tpu_custom_call" | custom-call | tf_op jit(solution)/shard_map/pallas_call | solution.py:334
  85.4 0.8 copy.14
  86.2 0.7 copy.15
  86.9 0.7 copy.16
Async XLA Ops:
  0.6 2.3 %copy-start = (bf16[1,128,2048]{2,1,0:T(8,128)(2,1)S(1)}, bf16[1,128,2048]{2,1,0:T(8,128)(2,1)}, u32[]{:S(2)}) copy-start(bf16[1,128,2048]{2,1,0:T(8,128)(2,1)} %param.8) | copy-start | bytes 1572868
  0.6 2.3 %copy-start.1 = (bf16[1,128,512]{2,1,0:T(8,128)(2,1)S(1)}, bf16[1,128,512]{2,1,0:T(8,128)(2,1)}, u32[]{:S(2)}) copy-start(bf16[1,128,512]{2,1,0:T(8,128)(2,1)} %param.9) | copy-start | bytes 393220
  0.7 2.3 %copy-start.2 = (bf16[1,128,512]{2,1,0:T(8,128)(2,1)S(1)}, bf16[1,128,512]{2,1,0:T(8,128)(2,1)}, u32[]{:S(2)}) copy-start(bf16[1,128,512]{2,1,0:T(8,128)(2,1)} %param.10) | copy-start | bytes 393220
  0.7 2.3 %copy-start.3 = (f32[1,16,128]{2,1,0:T(8,128)S(1)}, f32[1,16,128]{2,1,0:T(8,128)}, u32[]{:S(2)}) copy-start(f32[1,16,128]{2,1,0:T(8,128)} %param.12) | copy-start | bytes 24580
  0.7 2.3 %copy-start.4 = (s32[4]{0:T(128)S(1)}, s32[4]{0:T(128)}, u32[]{:S(2)}) copy-start(s32[4]{0:T(128)} %lengths.1) | copy-start | bytes 52
  0.7 2.3 %copy-start.5 = (s32[1,3,1]{1,2,0:T(1,128)S(1)}, s32[1,3,1]{1,2,0:T(1,128)}, u32[]{:S(2)}) copy-start(s32[1,3,1]{1,2,0:T(1,128)} %param.15) | copy-start | bytes 40

commit v2 on v1

--- a/solution.py
+++ b/solution.py
@@ -38,6 +38,7 @@
 ):
     N = T * S
     ROWS = 128
+    mid = T // 2
     W = up_ref.shape[1]
     C = (KV * G * HD) // W
     shift = int(math.log2(N))
@@ -90,8 +91,24 @@
             (lax.rem(t + T - o, T), s),
         )
 
-    for o in range(1, T):
-        z_copy(o).start()
+    def near_in(o):
+        return (t != 0) if o == 1 else (t != T - 1) if o == T - 1 else (t >= 0)
+
+    order = (mid,) + tuple(o for o in range(1, T) if o != mid)
+    for o in order:
+        @pl.when(near_in(o))
+        def _():
+            z_copy(o).start()
+
+    inner = (t == 1) | (t == T - 2)
+
+    def z_pass():
+        low = t == 1
+        return remote(
+            sibc.at[mid - 1], sibc.at[jnp.where(low, T - 2, 0)],
+            z_send.at[T - 1], z_recv.at[jnp.where(low, T - 2, 0)],
+            (jnp.where(low, 0, T - 1), s),
+        )
 
     def kv_copy(d):
         return remote(kvall.at[s], kvall.at[s], kv_send.at[d], kv_recv.at[s], (t, d))
@@ -120,6 +137,11 @@
     @pl.when(s == 0)
     def _():
         sibp[...] = jnp.zeros_like(sibp)
+
+    @pl.when(inner)
+    def _():
+        z_copy(mid).wait_recv()
+        z_pass().start()
 
     whole = rows_in.at[pl.ds(0, (N - 1) * 16)]
     pltpu.make_async_copy(whole, whole, up_recv).wait()
@@ -188,7 +210,12 @@
         )
 
     for o in range(1, T):
-        z_copy(o).wait_recv()
+        if o == mid:
+            @pl.when(jnp.logical_not(inner))
+            def _():
+                z_copy(o).wait_recv()
+        else:
+            z_copy(o).wait_recv()
 
         @pl.when(s < S - 1)
         def _():
@@ -288,6 +315,10 @@
         dk_ref[:, g * HD:(g + 1) * HD] = acc[g].astype(BF16)
         dv_ref[:, g * HD:(g + 1) * HD] = acc[KV + g].astype(BF16)
 
+    @pl.when(inner)
+    def _():
+        z_pass().wait_send()
+
     sent = up_ref.at[pl.ds(0, (N - 1) * 16)]
     pltpu.make_async_copy(sent, sent, up_send).wait()
 
@@ -303,7 +334,10 @@
 
     lax.fori_loop(0, s, g_left, 0)
     for o in range(1, T):
-        z_copy(o).wait_send()
+        @pl.when(near_in(o))
+        def _():
+            z_copy(o).wait_send()
+
         y_copy(o).wait_send()
 
         @pl.when(s < S - 1)
@@ -358,7 +392,7 @@
             pltpu.VMEM((KV, 1, G * rows), F32),
             pltpu.VMEM((KV, G * rows, HD), F32),
             pltpu.VMEM(block, F32),
-            dma, dma, dma((S,)), dma((S,)), dma((T - 1,)), dma((T - 1,)),
+            dma, dma, dma((S,)), dma((S,)), dma((T,)), dma((T - 1,)),
             dma((T - 1,)), dma((T - 1,)), dma((S,)), dma((S,)),
             dma((T - 1,)), dma((T - 1,)), dma((T - 1,)), dma((T - 1,)),
         ],

time: 87.7 us -> 82.6 us (0.942)
  the two profiles are of different devices: /device:TPU:3 before, /device:TPU:11 now
where the time goes in v2:
time: 82.6 us; the launch traced here: 82.5 us
  Pallas kernels  77.4 us (94%)
  local copies, waits for them, and re-layouts  4.34 us (5%)
    pallas_call x1, Pallas kernels, shards(): pl.pallas_call(functools.partial(body, T, S, G, KV, HD), out_shape=(jax.S...  77.4 us
    reshape x1, local copies, waits for them, and re-layouts, shards(): up = upstream.reshape(N * 16, width)  2.21 us
    unnamed x15, local copies, waits for them, and re-layouts  2.13 us

profile of v2, /device:TPU:11, one launch (start us, length us, event | category | flops | bytes accessed | tf_op | source)
XLA Modules:
  0.0 82.5 jit_solution(10818166173500550799)
XLA Ops:
  0.6 0.0 copy-start
  0.6 0.0 copy-start.1
  0.7 0.0 copy-start.2
  0.7 0.0 copy-start.3
  0.7 0.0 copy-start.4
  0.7 0.0 copy-start.5
  0.7 2.2 %reshape.13.up_ref = bf16[512,512]{1,0:T(8,128)(2,1)} reshape(bf16[128,1,2048]{2,0,1:T(8,128)(2,1)} %param.13) | data formatting | bytes 1048576 | tf_op jit(solution)/shard_map/reshape | solution.py:363
  2.9 0.0 copy-done
  2.9 0.0 copy-done.1
  2.9 0.0 copy-done.2
  2.9 0.0 copy-done.3
  2.9 0.0 copy-done.4
  2.9 0.0 copy-done.5
  2.9 77.4 %shard_map.103 = (bf16[128,2048]{1,0:T(8,128)(2,1)S(1)}, bf16[128,512]{1,0:T(8,128)(2,1)S(1)}, bf16[128,512]{1,0:T(8,128)(2,1)S(1)}) custom-call(s32[4]{0:T(128)S(1)} %copy-done.4, s32[3]{0:T(128)S(1)} %bitcast.18, bf16[128,2048]{1,0:T(8,128)(2,1)S(1)} %bitcast.11, bf16[128,512]{1,0:T(8,128)(2,1)S(1)} %bitcast.13, bf16[128,512]{1,0:T(8,128)(2,1)S(1)} %bitcast.14, ...), custom_call_target="tpu_custom_call" | custom-call | tf_op jit(solution)/shard_map/pallas_call | solution.py:368
  80.4 0.8 copy.14
  81.2 0.7 copy.15
  81.8 0.7 copy.16
Async XLA Ops:
  0.6 2.3 %copy-start = (bf16[1,128,2048]{2,1,0:T(8,128)(2,1)S(1)}, bf16[1,128,2048]{2,1,0:T(8,128)(2,1)}, u32[]{:S(2)}) copy-start(bf16[1,128,2048]{2,1,0:T(8,128)(2,1)} %param.8) | copy-start | bytes 1572868
  0.6 2.3 %copy-start.1 = (bf16[1,128,512]{2,1,0:T(8,128)(2,1)S(1)}, bf16[1,128,512]{2,1,0:T(8,128)(2,1)}, u32[]{:S(2)}) copy-start(bf16[1,128,512]{2,1,0:T(8,128)(2,1)} %param.9) | copy-start | bytes 393220
  0.7 2.3 %copy-start.2 = (bf16[1,128,512]{2,1,0:T(8,128)(2,1)S(1)}, bf16[1,128,512]{2,1,0:T(8,128)(2,1)}, u32[]{:S(2)}) copy-start(bf16[1,128,512]{2,1,0:T(8,128)(2,1)} %param.10) | copy-start | bytes 393220
  0.7 2.3 %copy-start.3 = (f32[1,16,128]{2,1,0:T(8,128)S(1)}, f32[1,16,128]{2,1,0:T(8,128)}, u32[]{:S(2)}) copy-start(f32[1,16,128]{2,1,0:T(8,128)} %param.12) | copy-start | bytes 24580
  0.7 2.3 %copy-start.4 = (s32[4]{0:T(128)S(1)}, s32[4]{0:T(128)}, u32[]{:S(2)}) copy-start(s32[4]{0:T(128)} %lengths.1) | copy-start | bytes 52
  0.7 2.3 %copy-start.5 = (s32[1,3,1]{1,2,0:T(1,128)S(1)}, s32[1,3,1]{1,2,0:T(1,128)}, u32[]{:S(2)}) copy-start(s32[1,3,1]{1,2,0:T(1,128)} %param.15) | copy-start | bytes 40

commit v3 on v2

--- a/solution.py
+++ b/solution.py
@@ -209,7 +209,7 @@
             (t, lax.rem(s + S - 1, S)),
         )
 
-    for o in range(1, T):
+    for o in order:
         if o == mid:
             @pl.when(jnp.logical_not(inner))
             def _():
@@ -221,7 +221,7 @@
         def _():
             shift_copy(o).start()
 
-    for o in range(1, T):
+    for o in order:
         @pl.when(s > 0)
         def _():
             shift_copy(o).wait_recv()
@@ -281,7 +281,7 @@
             (lax.rem(t + o, T), s),
         )
 
-    for o in range(1, T):
+    for o in order:
         @pl.when(s < S - 1)
         def _():
             back_copy(o).wait_recv()

time: 82.6 us -> 79.8 us (0.966)
  Pallas kernels: 77.4 us -> 74.6 us
    pallas_call x1, Pallas kernels: 77.4 us -> 74.6 us  [shards(): pl.pallas_call(functools.partial(body, T, S, G, KV, HD), out_shape=(jax.S...]
where the time goes in v3:
time: 79.8 us; the launch traced here: 79.7 us
  Pallas kernels  74.6 us (93%)
  local copies, waits for them, and re-layouts  4.34 us (5%)
    pallas_call x1, Pallas kernels, shards(): pl.pallas_call(functools.partial(body, T, S, G, KV, HD), out_shape=(jax.S...  74.6 us
    reshape x1, local copies, waits for them, and re-layouts, shards(): up = upstream.reshape(N * 16, width)  2.21 us
    unnamed x15, local copies, waits for them, and re-layouts  2.13 us

profile of v3, /device:TPU:11, one launch (start us, length us, event | category | flops | bytes accessed | tf_op | source)
XLA Modules:
  0.0 79.7 jit_solution(1520006947642551101)
XLA Ops:
  0.6 0.0 copy-start
  0.6 0.0 copy-start.1
  0.7 0.0 copy-start.2
  0.7 0.0 copy-start.3
  0.7 0.0 copy-start.4
  0.7 0.0 copy-start.5
  0.7 2.2 %reshape.13.up_ref = bf16[512,512]{1,0:T(8,128)(2,1)} reshape(bf16[128,1,2048]{2,0,1:T(8,128)(2,1)} %param.13) | data formatting | bytes 1048576 | tf_op jit(solution)/shard_map/reshape | solution.py:363
  2.9 0.0 copy-done
  2.9 0.0 copy-done.1
  2.9 0.0 copy-done.2
  2.9 0.0 copy-done.3
  2.9 0.0 copy-done.4
  2.9 0.0 copy-done.5
  2.9 74.6 %shard_map.103 = (bf16[128,2048]{1,0:T(8,128)(2,1)S(1)}, bf16[128,512]{1,0:T(8,128)(2,1)S(1)}, bf16[128,512]{1,0:T(8,128)(2,1)S(1)}) custom-call(s32[4]{0:T(128)S(1)} %copy-done.4, s32[3]{0:T(128)S(1)} %bitcast.18, bf16[128,2048]{1,0:T(8,128)(2,1)S(1)} %bitcast.11, bf16[128,512]{1,0:T(8,128)(2,1)S(1)} %bitcast.13, bf16[128,512]{1,0:T(8,128)(2,1)S(1)} %bitcast.14, ...), custom_call_target="tpu_custom_call" | custom-call | tf_op jit(solution)/shard_map/pallas_call | solution.py:368
  77.6 0.8 copy.14
  78.4 0.7 copy.15
  79.0 0.7 copy.16
Async XLA Ops:
  0.6 2.3 %copy-start = (bf16[1,128,2048]{2,1,0:T(8,128)(2,1)S(1)}, bf16[1,128,2048]{2,1,0:T(8,128)(2,1)}, u32[]{:S(2)}) copy-start(bf16[1,128,2048]{2,1,0:T(8,128)(2,1)} %param.8) | copy-start | bytes 1572868
  0.6 2.3 %copy-start.1 = (bf16[1,128,512]{2,1,0:T(8,128)(2,1)S(1)}, bf16[1,128,512]{2,1,0:T(8,128)(2,1)}, u32[]{:S(2)}) copy-start(bf16[1,128,512]{2,1,0:T(8,128)(2,1)} %param.9) | copy-start | bytes 393220
  0.7 2.3 %copy-start.2 = (bf16[1,128,512]{2,1,0:T(8,128)(2,1)S(1)}, bf16[1,128,512]{2,1,0:T(8,128)(2,1)}, u32[]{:S(2)}) copy-start(bf16[1,128,512]{2,1,0:T(8,128)(2,1)} %param.10) | copy-start | bytes 393220
  0.7 2.3 %copy-start.3 = (f32[1,16,128]{2,1,0:T(8,128)S(1)}, f32[1,16,128]{2,1,0:T(8,128)}, u32[]{:S(2)}) copy-start(f32[1,16,128]{2,1,0:T(8,128)} %param.12) | copy-start | bytes 24580
  0.7 2.3 %copy-start.4 = (s32[4]{0:T(128)S(1)}, s32[4]{0:T(128)}, u32[]{:S(2)}) copy-start(s32[4]{0:T(128)} %lengths.1) | copy-start | bytes 52
  0.7 2.3 %copy-start.5 = (s32[1,3,1]{1,2,0:T(1,128)S(1)}, s32[1,3,1]{1,2,0:T(1,128)}, u32[]{:S(2)}) copy-start(s32[1,3,1]{1,2,0:T(1,128)} %param.15) | copy-start | bytes 40

commit v4 on v3

--- a/solution.py
+++ b/solution.py
@@ -138,10 +138,21 @@
     def _():
         sibp[...] = jnp.zeros_like(sibp)
 
+    def shift_copy(o):
+        return remote(
+            sibc.at[o - 1], sibp.at[o - 1], h_send.at[o - 1], h_recv.at[o - 1],
+            (t, lax.rem(s + 1, S)),
+        )
+
+    z_copy(mid).wait_recv()
+
     @pl.when(inner)
     def _():
-        z_copy(mid).wait_recv()
         z_pass().start()
+
+    @pl.when(s < S - 1)
+    def _():
+        shift_copy(mid).start()
 
     whole = rows_in.at[pl.ds(0, (N - 1) * 16)]
     pltpu.make_async_copy(whole, whole, up_recv).wait()
@@ -195,27 +206,14 @@
 
         lax.fori_loop(0, KV, step, 0)
 
-    own(s, True)
-
-    def shift_copy(o):
-        return remote(
-            sibc.at[o - 1], sibp.at[o - 1], h_send.at[o - 1], h_recv.at[o - 1],
-            (t, lax.rem(s + 1, S)),
-        )
-
     def back_copy(o):
         return remote(
             gsp.at[o - 1], gspr.at[o - 1], b_send.at[o - 1], b_recv.at[o - 1],
             (t, lax.rem(s + S - 1, S)),
         )
 
-    for o in order:
-        if o == mid:
-            @pl.when(jnp.logical_not(inner))
-            def _():
-                z_copy(o).wait_recv()
-        else:
-            z_copy(o).wait_recv()
+    for o in order[1:]:
+        z_copy(o).wait_recv()
 
         @pl.when(s < S - 1)
         def _():
@@ -272,6 +270,7 @@
         g_copy(b).start()
         return c
 
+    own(s, True)
     half = s // 2
     lax.fori_loop(0, half, own_step, 0)
 

time: 79.8 us -> 80.3 us (level)
  no operation moved by 1% of the time
where the time goes in v4:
time: 80.3 us; the launch traced here: 80.1 us
  Pallas kernels  75.1 us (94%)
  local copies, waits for them, and re-layouts  4.34 us (5%)
    pallas_call x1, Pallas kernels, shards(): pl.pallas_call(functools.partial(body, T, S, G, KV, HD), out_shape=(jax.S...  75.1 us
    reshape x1, local copies, waits for them, and re-layouts, shards(): up = upstream.reshape(N * 16, width)  2.21 us
    unnamed x15, local copies, waits for them, and re-layouts  2.13 us

profile of v4, /device:TPU:11, one launch (start us, length us, event | category | flops | bytes accessed | tf_op | source)
XLA Modules:
  0.0 80.1 jit_solution(797806922153239213)
XLA Ops:
  0.6 0.0 copy-start
  0.6 0.0 copy-start.1
  0.7 0.0 copy-start.2
  0.7 0.0 copy-start.3
  0.7 0.0 copy-start.4
  0.7 0.0 copy-start.5
  0.7 2.2 %reshape.13.up_ref = bf16[512,512]{1,0:T(8,128)(2,1)} reshape(bf16[128,1,2048]{2,0,1:T(8,128)(2,1)} %param.13) | data formatting | bytes 1048576 | tf_op jit(solution)/shard_map/reshape | solution.py:362
  2.9 0.0 copy-done
  2.9 0.0 copy-done.1
  2.9 0.0 copy-done.2
  2.9 0.0 copy-done.3
  2.9 0.0 copy-done.4
  2.9 0.0 copy-done.5
  2.9 75.1 %shard_map.103 = (bf16[128,2048]{1,0:T(8,128)(2,1)S(1)}, bf16[128,512]{1,0:T(8,128)(2,1)S(1)}, bf16[128,512]{1,0:T(8,128)(2,1)S(1)}) custom-call(s32[4]{0:T(128)S(1)} %copy-done.4, s32[3]{0:T(128)S(1)} %bitcast.18, bf16[128,2048]{1,0:T(8,128)(2,1)S(1)} %bitcast.11, bf16[128,512]{1,0:T(8,128)(2,1)S(1)} %bitcast.13, bf16[128,512]{1,0:T(8,128)(2,1)S(1)} %bitcast.14, ...), custom_call_target="tpu_custom_call" | custom-call | tf_op jit(solution)/shard_map/pallas_call | solution.py:367
  78.0 0.8 copy.14
  78.8 0.7 copy.15
  79.5 0.7 copy.16
Async XLA Ops:
  0.6 2.3 %copy-start = (bf16[1,128,2048]{2,1,0:T(8,128)(2,1)S(1)}, bf16[1,128,2048]{2,1,0:T(8,128)(2,1)}, u32[]{:S(2)}) copy-start(bf16[1,128,2048]{2,1,0:T(8,128)(2,1)} %param.8) | copy-start | bytes 1572868
  0.6 2.3 %copy-start.1 = (bf16[1,128,512]{2,1,0:T(8,128)(2,1)S(1)}, bf16[1,128,512]{2,1,0:T(8,128)(2,1)}, u32[]{:S(2)}) copy-start(bf16[1,128,512]{2,1,0:T(8,128)(2,1)} %param.9) | copy-start | bytes 393220
  0.7 2.3 %copy-start.2 = (bf16[1,128,512]{2,1,0:T(8,128)(2,1)S(1)}, bf16[1,128,512]{2,1,0:T(8,128)(2,1)}, u32[]{:S(2)}) copy-start(bf16[1,128,512]{2,1,0:T(8,128)(2,1)} %param.10) | copy-start | bytes 393220
  0.7 2.3 %copy-start.3 = (f32[1,16,128]{2,1,0:T(8,128)S(1)}, f32[1,16,128]{2,1,0:T(8,128)}, u32[]{:S(2)}) copy-start(f32[1,16,128]{2,1,0:T(8,128)} %param.12) | copy-start | bytes 24580
  0.7 2.3 %copy-start.4 = (s32[4]{0:T(128)S(1)}, s32[4]{0:T(128)}, u32[]{:S(2)}) copy-start(s32[4]{0:T(128)} %lengths.1) | copy-start | bytes 52
  0.7 2.3 %copy-start.5 = (s32[1,3,1]{1,2,0:T(1,128)S(1)}, s32[1,3,1]{1,2,0:T(1,128)}, u32[]{:S(2)}) copy-start(s32[1,3,1]{1,2,0:T(1,128)} %param.15) | copy-start | bytes 40
